TPU v7x, 128 devices: a whole 4x4x4 slice. The times are simulated.
128 devices in a mesh: group: 8 (over y_hi, z), member: 16 (over y_lo, x, core).
Axes of the slice: x: 4, y: 4 (y_hi: 2, y_lo: 2; y = y_hi * 2 + y_lo), z: 4, core: 2. Of those that a mesh axis runs over, the one named last changes fastest.
Arguments:
- embeddings: bfloat16 [16, 8192, 1024], P('group', 'member')
- order_rank: int32 [16, 8192], P('group', 'member'), may hold values from 0 to 8191, each once within a row
- lengths: int32 [16], P('group'), may hold values from 1 to 8192, 65536 in all
Outputs:
- highest: float32 [16, 8192], P('group', 'member')
Inputs may be any that keep to these rules, and one draw needn't show every extreme that they name: `order_rank`: the ranks of one cluster are distinct.
All inputs are finite; a program needn't handle non-finite values. No bound on the sum of `lengths` on one device may be relied on, other than what follows from the above.
Results may differ from a plain program's by a relative error of at most 0.0003.
Values may be sent and summed in bfloat16 or wider, within the bound.
A program may use at most 128 MiB of HBM per device.

v0:
```python
import jax
import jax.numpy as jnp
from jax import lax
from jax.sharding import PartitionSpec as P


def local(embeddings, order_rank, lengths):
    clusters_here = embeddings.shape[0]
    slots_here = embeddings.shape[1]
    position = lax.axis_index("member")
    own_first = position * slots_here
    slots = own_first + jnp.arange(slots_here, dtype=jnp.int32)
    is_live = slots[None, :] < lengths[:, None]
    values = embeddings.astype(jnp.float32)
    summed = jnp.sum(jnp.where(is_live[:, :, None], values, 0.0), axis=(0, 1))
    counted = jnp.sum(is_live.astype(jnp.float32))
    summed, counted = lax.psum((summed, counted), ("group", "member"))
    center = summed / counted
    shifted = values - center
    normed = (
        shifted * lax.rsqrt(jnp.sum(shifted * shifted, axis=-1, keepdims=True) + 1e-06)
    ).astype(jnp.bfloat16)
    all_ranks = lax.all_gather(order_rank, "member", axis=1, tiled=True)
    start_best = jnp.full((clusters_here, slots_here), -1.0, jnp.float32)
    block_rows = lax.all_gather(normed, "member", axis=1, tiled=True)
    width = block_rows.shape[1]
    cosines = jnp.einsum("csd,cpd->csp", normed, block_rows, preferred_element_type=jnp.float32)
    col_live = jnp.arange(width, dtype=jnp.int32)[None, :] < lengths[:, None]
    allowed = col_live[:, None, :] & (all_ranks[:, None, :] < order_rank[:, :, None])
    own_best = jnp.max(jnp.where(allowed, cosines, -1.0), axis=2)
    running = jnp.maximum(start_best, own_best)
    return jnp.where(is_live, running, -1.0)


def solution(mesh):
    placed = (P("group", "member", None), P("group", "member"), P("group"))
    return jax.shard_map(
        local, mesh=mesh, in_specs=placed, out_specs=P("group", "member"), check_vma=False
    )
```

profile of v0, /device:TPU:1, one launch (start us, length us, event | category | flops | bytes accessed | tf_op | source)
XLA Modules:
  0.0 283.1 jit_solution(12174460583617138738)
XLA Ops:
  6.5 0.0 copy-start
  6.5 0.0 all-gather.2.cloned.1.call-start
  6.5 1.5 convert_reduce_fusion
  8.0 2.1 fusion.4
  10.1 68.9 %all-reduce = (f32[1024]{0:T(1024)S(1)}, f32[]{:T(128)}) all-reduce(f32[1024]{0:T(1024)S(1)} %fusion.4, f32[]{:T(128)} %get-tuple-element.7), channel_id=1, replica_groups=mesh['group'=8,'member'=16] {'group','member'}, use_global_device_ids=true, to_apply=%region_1.2 | all-reduce | flops 1025 | bytes 8200 | tf_op jit(solution)/shard_map/psum | solution.py:17
  79.0 0.6 broadcast_divide_fusion
  79.6 0.0 copy-start.1
  79.6 0.0 copy-start.2
  79.7 2.2 fusion.2
  81.9 0.0 copy-done
  81.9 1.8 fusion.3
  83.7 0.0 all-gather.2.cloned.1.call-update
  83.8 0.0 copy-done.1
  83.8 18.6 %all_gather.6 = s32[2,8192]{1,0:T(2,128)S(1)} all-gather(s32[2,512]{1,0:T(2,128)S(1)} %copy-done.1), channel_id=1, replica_groups=mesh['group'=8,'member'=16] {'member'}, dimensions={1}, use_global_device_ids=true | all-gather | bytes 69632 | tf_op jit(solution)/shard_map/all_gather | solution.py:23
  102.4 0.0 copy-done.2
  102.4 0.1 iota_compare_fusion
  102.5 149.1 %all-gather.2.cloned.1.call-done = bf16[2,8192,1024]{2,1,0:T(8,128)(2,1)} async-done(((bf16[2,512,1024]{2,1,0:T(8,128)(2,1)}), bf16[2,8192,1024]{2,1,0:T(8,128)(2,1)}) %all-gather.2.cloned.1.call-update) | async-done | bytes 33554448 | tf_op jit(solution)/shard_map/all_gather | solution.py:25
  251.5 24.1 %select_reduce_fusion = f32[2,512]{1,0:T(2,128)S(1)} fusion(s32[2,512]{1,0:T(2,128)S(1)} %copy-done.1, s32[2,8192]{1,0:T(2,128)S(1)} %all_gather.6, pred[2,8192]{1,0:T(4,128)(4,1)S(1)} %iota_compare_fusion, bf16[2,512,1024]{2,1,0:T(8,128)(2,1)} %fusion.3, bf16[2,8192,1024]{2,1,0:T(8,128)(2,1)} %all-gather.2.cloned.1.call-done), kind=kOutput, calls=%fused_computation | convolution fusion | flops 17213423616 | bytes 35741696 | tf_op jit(solution)/shard_map/csd,cpd->csp/dot_general | solution.py:27
  275.7 0.6 maximum_select_fusion
  (2 shorter events, 0.0 us)
Async XLA Ops:
  6.5 75.4 %copy-start = (bf16[2,512,1024]{2,1,0:T(8,128)(2,1)S(1)}, bf16[2,512,1024]{2,1,0:T(8,128)(2,1)}, u32[]{:S(2)}) copy-start(bf16[2,512,1024]{2,1,0:T(8,128)(2,1)} %param.3) | copy-start | bytes 6291460
  6.5 245.0 %all-gather.2.cloned.1.call-start = ((), (), s32[]{:S(2)}) async-start(), calls=%async_computation | async-start | bytes 35651584 | tf_op jit(solution)/shard_map/all_gather | solution.py:25
  79.6 4.1 %copy-start.1 = (s32[2,512]{1,0:T(2,128)S(1)}, s32[2,512]{1,0:T(2,128)}, u32[]{:S(2)}) copy-start(s32[2,512]{1,0:T(2,128)} %param.4) | copy-start | bytes 12292
  79.6 22.7 %copy-start.2 = (s32[2]{0:T(128)S(1)}, s32[2]{0:T(128)}, u32[]{:S(2)}) copy-start(s32[2]{0:T(128)} %param.5) | copy-start | bytes 28
Sparse Core Ops, SparseCore 0:
  83.9 167.6 all-gather.1
where the time goes:
time: 283 us
  waiting for transfers between devices  149 us (53%)
  blocking collectives  87.5 us (31%)
  matrix products  24.1 us (9%)
  between operations  13.4 us (5%)
  other arithmetic  8.99 us (3%)
    all_gather x1, waiting for transfers between devices, local(): block_rows = lax.all_gather(normed, 'member', axis=1, tiled=True)  149 us
    psum x1, blocking collectives, local(): summed, counted = lax.psum((summed, counted), ('group', 'member'))  68.9 us
    dot_general x1, matrix products, local(): jnp.einsum('csd,cpd->csp', normed, block_rows, preferred_element_type=jnp...  24.1 us
    all_gather x1, blocking collectives, local(): all_ranks = lax.all_gather(order_rank, 'member', axis=1, tiled=True)  18.6 us
  transfers between devices with their start and end apart: 1, of which 1 were waited for; matrix products, arithmetic and copies ran while one was open for 0% of the time, Pallas kernels for 0%

commit v1 on v0

v1 whole, which is shorter than its diff:
```python
import functools

import jax
import jax.numpy as jnp
from jax import lax
from jax.experimental import pallas as pl
from jax.experimental.pallas import tpu as pltpu
from jax.sharding import PartitionSpec as P

MESH = pl.DeviceIdType.MESH
UNIT = 128
PER = 4
STEPS = 6
LP, LQ, LR = 4, 10, 16
OTHER = 22
NO_RANK = 1e9
FILL, BULK = 8, 12
WIDE = 4
NONE = -1


def needed(role):
    own, q, r = (0, 2), (LQ, LQ + 2, LQ + 4), (LR, LR + 2, LR + 4)
    p = (LP + 2, LP + 4) if role == 2 else (LP, LP + 2)
    columns = lambda firsts: [u + i for u in firsts for i in range(2)]
    jobs = []
    if role == 2:
        jobs += [(u, v) for u in own + r[:2] for v in columns(q)]
        jobs += [(u, v) for u in p for v in columns(q[2:])] + [(u, v) for u in q[:2] for v in columns(p)]
        jobs += [(u, v) for u in q for v in columns(q) if v >= u]
        jobs += [(u, v) for u in own for v in columns(own) if v >= u]
        jobs += [(u, v) for u in own for v in columns(r[:2])]
        jobs += [(r[0], v) for v in columns(r[:2])]
    else:
        jobs += [(u, v) for u in own + p for v in columns(q + r)]
        if role == 0:
            for a in range(3):
                for b in range(3):
                    jobs += [(q[a], v) for v in columns([r[b]])] if b >= a else [(r[b], v) for v in columns([q[a]])]
        else:
            jobs += [(u, v) for u in own + p for v in columns(own + p) if v >= u]
            jobs += [(u, v) for u in q[:2] for v in columns(r[:2])]
    return jobs


def jobs_of(role):
    def there(unit):
        return 0 if unit < LP else (unit - LP) % STEPS + 1

    todo = sorted(needed(role), key=lambda job: max(there(job[0] + 1), there(job[1])))
    ready = lambda job: max(there(job[0] + 1), there(job[1]))
    plan, at = [], 0
    for stage in range(STEPS + 1):
        for limit, cap in ((stage - 1, FILL), (stage, BULK)):
            if stage == STEPS:
                cap = len(todo)
            take = []
            while at < len(todo) and ready(todo[at]) <= limit and len(take) < cap:
                take.append(todo[at])
                at += 1
            plan.append(take)
    return plan


def pick(index, values):
    out = jnp.int32(values[0])
    for i in range(1, len(values)):
        out = jnp.where(index == i, values[i], out)
    return out


def kernel(
    groups, lengths_hbm, emb, order_hbm, out, lengths, order, raw, norm, cranks, rranks, rowacc, colacc, sums, totals, ret, back, center,
    load_sem, raw_send, raw_recv, core_send, core_recv, sum_send, sum_recv, total_send, total_recv, ret_send, ret_recv,
):
    group, member = lax.axis_index("group"), lax.axis_index("member")
    core, x, y = member % 2, (member // 2) % 4, member // 8
    role = (x + 2 * y) % 4
    is_m = jnp.where(role == 3, 1, 0)
    mine = y + is_m * (1 - 2 * y)
    chip = 4 * y + x
    sibling = {"member": 2 * chip + 1 - core}

    def actual(c):
        cx, cy = c % 4, c // 4
        return (cx + 2 * mine) % 4 + 4 * (cy + mine * (1 - 2 * cy))

    xp, xm, yy = 4 * y + (x + 1) % 4, 4 * y + (x + 3) % 4, 4 * (1 - y) + x
    neighbour = [
        jnp.where(role == 0, xp, jnp.where(role == 3, yy, xm)),
        jnp.where((role == 1) | (role == 2), xp, xm),
        jnp.where(role == 3, xp, yy),
    ]
    bases = (LP, LQ, LR)
    landing = [
        pick(role, (LP, LP, LQ, LR)),
        pick(role, (LR, LP, LQ, LQ)),
        pick(role, (LR, LP, LR, LQ)),
    ]
    late_pair = role >= 2

    small = [
        pltpu.make_async_copy(lengths_hbm, lengths, load_sem.at[2]),
        pltpu.make_async_copy(order_hbm, order, load_sem.at[3]),
    ]
    for cp in small:
        cp.start()
    loads = []
    for i, (cluster, first) in enumerate(((mine, 0), (1 - mine, OTHER))):
        loads.append(pltpu.make_async_copy(emb.at[cluster], raw.at[pl.ds(first, PER)], load_sem.at[i]))
        loads[-1].start()
    barrier = pltpu.get_barrier_semaphore()
    for i in range(1, 16):
        pl.semaphore_signal(barrier, inc=1, device_id={"member": (member + i) % 16}, device_id_type=MESH)
    for i in range(1, groups):
        pl.semaphore_signal(barrier, inc=1, device_id={"group": (group + i) % groups}, device_id_type=MESH)

    rowacc[...] = jnp.full(rowacc.shape, -1.0, jnp.float32)
    colacc[...] = jnp.full(colacc.shape, -1.0, jnp.float32)
    ret[...] = jnp.full(ret.shape, -1.0, jnp.float32)
    back[...] = jnp.full(back.shape, -1.0, jnp.float32)

    for cp in small:
        cp.wait()
    first_slot = member * (PER * UNIT)
    lane = lax.broadcasted_iota(jnp.int32, (1, UNIT), 1)
    own_ranks, own_live = [], []
    for c in range(2):
        for i in range(PER):
            is_live = first_slot + i * UNIT + lane < lengths[c]
            own_live.append(is_live)
            own = order[c : c + 1, i * UNIT : (i + 1) * UNIT].astype(jnp.float32)
            own_ranks.append(jnp.where(is_live, own, NO_RANK))
    sums[member, 16:24, :] = jnp.concatenate(own_ranks, axis=0)

    for cp in loads:
        cp.wait()
    row = lax.broadcasted_iota(jnp.int32, (UNIT, 1), 0)

    def add_unit(i, carry):
        total, count = carry
        other = i // PER
        cluster = mine + other * (1 - 2 * mine)
        at = i % PER
        is_live = first_slot + at * UNIT + row < lengths[cluster]
        values = jnp.where(is_live, raw[at + other * OTHER].astype(jnp.float32), 0.0)
        total = total + jnp.sum(values.reshape(UNIT // 8, 8, -1), axis=0)
        count = count + jnp.sum(is_live.astype(jnp.float32), axis=0, keepdims=True)
        return total, count

    total, count = lax.fori_loop(0, 2 * PER, add_unit, (jnp.zeros((8, 1024), jnp.float32), jnp.zeros((1, 1), jnp.float32)))
    total = jnp.sum(total, axis=0, keepdims=True)
    rows_out = [total[:, 128 * i : 128 * (i + 1)] for i in range(8)]
    rows_out += [jnp.broadcast_to(count, (1, 128))] + [jnp.zeros((7, 128), jnp.float32)]
    sums[member, 0:16, :] = jnp.concatenate(rows_out, axis=0)

    pl.semaphore_wait(barrier, 15 + groups - 1)

    def to_member(buffer, send, recv, i):
        return pltpu.make_async_remote_copy(
            src_ref=buffer.at[member], dst_ref=buffer.at[member], send_sem=send.at[i], recv_sem=recv.at[member],
            device_id={"member": (member + i) % 16}, device_id_type=MESH,
        )

    def from_member(buffer, send, recv, i):
        source = (member + 16 - i) % 16
        return pltpu.make_async_remote_copy(
            src_ref=buffer.at[source], dst_ref=buffer.at[source], send_sem=send.at[i], recv_sem=recv.at[source],
            device_id={"member": (member + i) % 16}, device_id_type=MESH,
        )

    for i in range(1, 16):
        to_member(sums, sum_send, sum_recv, i).start()

    def source_of(link, s):
        if link == 0:
            return s if s < 4 else LR + s - 4
        by_c = (OTHER + (2 if link == 1 else 0) + s) if s < 2 else ((LR if link == 1 else LQ) + s - 2)
        by_h = OTHER + ((s + 2) % 4 if link == 1 else s % 4)
        by_lm = OTHER + s if s < 4 else LP + s - 4
        return pick(role, (by_h, by_c, by_lm, by_lm))

    def goes(link, s):
        if s < 4:
            return None
        return late_pair if link == 0 else role != 0

    def outgoing(link, s):
        return pltpu.make_async_remote_copy(
            src_ref=raw.at[source_of(link, s)], dst_ref=raw.at[landing[link] + s],
            send_sem=raw_send.at[link, s], recv_sem=raw_recv.at[landing[link] - LP + s],
            device_id={"member": 2 * neighbour[link] + core}, device_id_type=MESH,
        )

    def arriving(link, s):
        unit = bases[link] + s
        return pltpu.make_async_remote_copy(
            src_ref=raw.at[unit], dst_ref=raw.at[unit], send_sem=raw_send.at[link, s], recv_sem=raw_recv.at[unit - LP],
            device_id={"member": 2 * neighbour[link] + core}, device_id_type=MESH,
        )

    def comes(link, s):
        if s < 4 or link == 1:
            return None
        return late_pair if link == 0 else jnp.logical_not(late_pair)

    def guarded(condition, do):
        if condition is None:
            do()
        else:
            pl.when(condition)(do)

    is_c = role == 1

    def send_step(s, everyone):
        for link in range(3):
            condition = None if everyone or link == 0 else jnp.logical_not(is_c)
            guarded(condition, lambda link=link: outgoing(link, s).start())

    def forward(s):
        if s == 0:
            send_step(1, True)
        if s + 2 < 4:
            send_step(s + 2, False)
        if s in (2, 3):

            @pl.when(late_pair)
            def _():
                for link in range(3):
                    outgoing(link, s + 2).start()

        if s < 4:

            @pl.when(is_c)
            def _():
                for link in (1, 2):
                    outgoing(link, s + 2).start()

    def arrive(s):
        for link in range(3):
            guarded(comes(link, s), lambda link=link: arriving(link, s).wait_recv())
        forward(s)

    send_step(0, True)

    for i in range(1, 16):
        from_member(sums, sum_send, sum_recv, i).wait_recv()
    totals[group] = jnp.sum(sums[:, 0:16, :], axis=0)

    def across(i, source):
        at = (group + groups - i) % groups if source else group
        return pltpu.make_async_remote_copy(
            src_ref=totals.at[at], dst_ref=totals.at[at], send_sem=total_send.at[i], recv_sem=total_recv.at[at],
            device_id={"group": (group + i) % groups}, device_id_type=MESH,
        )

    for i in range(1, groups):
        across(i, False).start()

    def owner_of(link, s):
        if link == 0:
            return actual(pick(role, (1, 0, 5, 2))), (s - 2 * jnp.where(late_pair, 1, 0))
        if link == 1:
            if s < 4:
                return actual(pick(role, (3, 2, 3, 4))), s
            return actual(pick(role, (7, 6, 7, 7))), s - 4 + 2 * is_m
        if s < 4:
            return actual(pick(role, (4, 5, 6, 6))), (s + 2 * is_m) % 4
        return actual(pick(role, (7, 6, 7, 7))), s - 2

    def set_ranks(unit, owner, at):
        line = 4 * mine + at
        both = [sums[2 * owner + j, pl.ds(16 + line, 1), :] for j in range(2)]
        cranks[unit] = jnp.concatenate(both, axis=1)
        own = sums[2 * owner + core, pl.ds(16 + line, 1), :]
        rranks[unit] = jnp.broadcast_to(own, (UNIT, UNIT)).T

    arrive(0)
    for i in range(PER):
        set_ranks(i, chip, i)
    for link in range(3):
        for s in range(STEPS):
            unit = bases[link] + s

            def one(link=link, s=s, unit=unit):
                set_ranks(unit, *owner_of(link, s))

            condition = comes(link, s)
            if link == 0 and s < 2:
                condition = jnp.logical_not(late_pair)
            guarded(condition, one)

    for i in range(1, groups):
        across(i, True).wait_recv()
    whole = jnp.sum(totals[...], axis=0)
    mean = whole[0:8] / whole[8:9]
    center[...] = jnp.concatenate([mean[i : i + 1] for i in range(8)], axis=1)

    half = pl.ds(pl.multiple_of(core * UNIT, UNIT), UNIT)
    theirs = pl.ds(pl.multiple_of((1 - core) * UNIT, UNIT), UNIT)

    def normalise(unit):
        shifted = raw[unit].astype(jnp.float32) - center[...]
        scale = lax.rsqrt(jnp.sum(shifted * shifted, axis=-1, keepdims=True) + 1e-06)
        norm[unit, half, :] = (shifted * scale).astype(jnp.bfloat16)

    def exchange(unit, rows):
        return pltpu.make_async_remote_copy(
            src_ref=norm.at[unit, rows], dst_ref=norm.at[unit, rows], send_sem=core_send.at[unit], recv_sem=core_recv.at[unit],
            device_id=sibling, device_id_type=MESH,
        )

    def prepare(unit):
        normalise(unit)
        exchange(unit, half).start()

    def pair(u, v):
        rows = norm[pl.ds(u, 2), half, :].reshape(2 * UNIT, 1024)
        cosines = lax.dot_general(rows, norm[v], (((1,), (1,)), ((), ())), preferred_element_type=jnp.float32)
        own = rranks[pl.ds(u, 2)].reshape(2 * UNIT, UNIT)
        best_rows = rowacc[pl.ds(u, 2)].reshape(2 * UNIT, UNIT)
        for h in range(2):
            at = slice(UNIT * h, UNIT * (h + 1))
            part, other = cosines[:, at], cranks[v, :, at]
            best_rows = jnp.maximum(best_rows, jnp.where(other < own, part, -1.0))
            up = jnp.where(own < other, part, -1.0)
            colacc[v, :, at] = jnp.maximum(colacc[v, :, at], jnp.max(up.reshape(2 * UNIT // 8, 8, UNIT), axis=0))
        rowacc[pl.ds(u, 2)] = best_rows.reshape(2, UNIT, UNIT)

    plans = [jobs_of(r) for r in range(3)]

    def run_jobs(part):
        lists = [plan[part] + plan[part][-1:] * (-len(plan[part]) % WIDE) for plan in plans]
        lists.append(lists[2])
        longest = max(len(jobs) for jobs in lists)
        if not longest:
            return
        codes = []
        for j in range(longest):
            at = [jobs[j][0] * 32 + jobs[j][1] if j < len(jobs) else 0 for jobs in lists]
            codes.append(pick(role, at))

        def body(j, _):
            for k in range(WIDE):
                code = codes[k]
                for i in range(1, longest // WIDE):
                    code = jnp.where(j == i, codes[WIDE * i + k], code)
                pair(code // 32, code % 32)
            return 0

        lax.fori_loop(0, pick(role, [len(jobs) // WIDE for jobs in lists]), body, 0)

    def held(link, s):
        if link == 0 and s < 2:
            return jnp.logical_not(late_pair)
        return comes(link, s)

    def own_unit(unit, _):
        prepare(unit)
        return 0

    lax.fori_loop(0, PER, own_unit, 0)
    arrive(1)
    for i in range(PER):
        exchange(i, theirs).wait_recv()
    run_jobs(1)
    for s in range(STEPS):
        if s > 1:
            arrive(s)
        for link in range(3):
            guarded(held(link, s), lambda link=link: prepare(bases[link] + s))
        run_jobs(2 * s + 2)
        for link in range(3):
            guarded(held(link, s), lambda link=link: exchange(bases[link] + s, theirs).wait_recv())
        run_jobs(2 * s + 3)

    def finish(unit, slot, at):
        best = jnp.max(colacc[unit], axis=0, keepdims=True)
        across_lanes = jnp.max(rowacc[unit].T, axis=0, keepdims=True)
        for j in range(2):
            part = best[:, UNIT * j : UNIT * (j + 1)]
            ret[slot, j, pl.ds(at, 1), :] = jnp.where(core == j, jnp.maximum(part, across_lanes), part)

    for link in range(3):
        for s in range(STEPS):
            slot = 1 + link if s < 4 or link == 0 else 4
            guarded(held(link, s), lambda link=link, s=s, slot=slot: finish(bases[link] + s, slot, owner_of(link, s)[1]))
    owners = [owner_of(0, 2)[0], owner_of(1, 0)[0], owner_of(2, 0)[0], owner_of(1, 4)[0]]

    def give(slot, j):
        return pltpu.make_async_remote_copy(
            src_ref=ret.at[slot, j], dst_ref=back.at[2 * chip + core], send_sem=ret_send.at[slot, j], recv_sem=ret_recv.at[2 * chip + core],
            device_id={"member": 2 * owners[slot - 1] + j}, device_id_type=MESH,
        )

    for slot in range(1, 5):
        for j in range(2):
            give(slot, j).start()
    for i in range(PER):
        finish(i, 0, i)
    to_sibling = pltpu.make_async_remote_copy(
        src_ref=ret.at[0, 1 - core], dst_ref=back.at[member], send_sem=ret_send.at[0, 0], recv_sem=ret_recv.at[member],
        device_id=sibling, device_id_type=MESH,
    )
    to_sibling.start()

    other_of = lambda c: (c % 4 + 2) % 4 + 4 * (1 - c // 4)
    givers = [
        actual(pick(role, (1, 0, 1, 1))),
        jnp.where(late_pair, actual(pick(role, (5, 5, 5, 2))), other_of(actual(pick(role, (1, 0, 0, 0))))),
        other_of(actual(pick(role, (2, 2, 0, 0)))),
        other_of(actual(pick(role, (5, 5, 5, 2)))),
    ]

    def take(source):
        return pltpu.make_async_remote_copy(
            src_ref=back.at[source], dst_ref=back.at[source], send_sem=ret_send.at[0, 1], recv_sem=ret_recv.at[source],
            device_id=sibling, device_id_type=MESH,
        )

    take(2 * chip + 1 - core).wait_recv()
    for giver in givers:
        for j in range(2):
            take(2 * giver + j).wait_recv()
    computes = lambda c: (c // 4) if c != 3 and c != 5 else 1 - c // 4
    for c in range(2):
        best = jnp.maximum(jnp.full((8, UNIT), -1.0, jnp.float32), jnp.where(mine == c, ret[0, core], -1.0))
        for source in range(16):
            if computes(source // 2) == c:
                best = jnp.maximum(best, back[source])
        for i in range(PER):
            out[c : c + 1, i * UNIT : (i + 1) * UNIT] = jnp.where(own_live[c * PER + i], best[i : i + 1], -1.0)

    for i in range(1, 16):
        to_member(sums, sum_send, sum_recv, i).wait_send()
    for i in range(1, groups):
        across(i, False).wait_send()
    for s in range(STEPS):
        for link in range(3):
            guarded(goes(link, s), lambda link=link: outgoing(link, s).wait_send())
    for i in range(PER):
        exchange(i, half).wait_send()
    for s in range(STEPS):
        for link in range(3):
            guarded(held(link, s), lambda link=link: exchange(bases[link] + s, half).wait_send())
    for slot in range(1, 5):
        for j in range(2):
            give(slot, j).wait_send()
    to_sibling.wait_send()


def solution(mesh):
    groups = mesh.shape["group"]
    units = LR + STEPS

    def local(embeddings, order_rank, lengths):
        d = embeddings.shape[-1]
        f32, dma = jnp.float32, pltpu.SemaphoreType.DMA
        return pl.pallas_call(
            functools.partial(kernel, groups),
            out_shape=jax.ShapeDtypeStruct(order_rank.shape, f32),
            in_specs=[
                pl.BlockSpec(memory_space=pl.ANY),
                pl.BlockSpec(memory_space=pl.ANY),
                pl.BlockSpec(memory_space=pl.ANY),
            ],
            out_specs=pl.BlockSpec(memory_space=pltpu.VMEM),
            scratch_shapes=[
                pltpu.SMEM(lengths.shape, jnp.int32),
                pltpu.VMEM(order_rank.shape, jnp.int32),
                pltpu.VMEM((OTHER + PER, UNIT, d), jnp.bfloat16),
                pltpu.VMEM((units, 2 * UNIT, d), jnp.bfloat16),
                pltpu.VMEM((units, 1, 2 * UNIT), f32),
                pltpu.VMEM((units, UNIT, UNIT), f32),
                pltpu.VMEM((units, UNIT, UNIT), f32),
                pltpu.VMEM((units, 8, 2 * UNIT), f32),
                pltpu.VMEM((16, 24, UNIT), f32),
                pltpu.VMEM((groups, 16, UNIT), f32),
                pltpu.VMEM((5, 2, 8, UNIT), f32),
                pltpu.VMEM((16, 8, UNIT), f32),
                pltpu.VMEM((1, d), f32),
                dma((4,)),
                dma((3, STEPS)),
                dma((3 * STEPS,)),
                dma((units,)),
                dma((units,)),
                dma((16,)),
                dma((16,)),
                dma((groups,)),
                dma((groups,)),
                dma((5, 2)),
                dma((16,)),
            ],
            compiler_params=pltpu.CompilerParams(collective_id=0, has_side_effects=True, vmem_limit_bytes=60 * 1024 * 1024),
            cost_estimate=pl.CostEstimate(flops=10_000_000_000, bytes_accessed=4_000_000, transcendentals=10_000),
        )(lengths, embeddings.reshape(2, PER, UNIT, d), order_rank)

    placed = (P("group", "member", None), P("group", "member"), P("group"))
    return jax.shard_map(local, mesh=mesh, in_specs=placed, out_specs=P("group", "member"), check_vma=False)
```

time: 283 us -> 63.3 us (0.22)
  waiting for transfers between devices: 149 us -> 0 us
  blocking collectives: 87.5 us -> 0 us
  Pallas kernels: 0 us -> 61.8 us
  matrix products: 24.1 us -> 0 us
  between operations: 13.4 us -> 0.01 us
  other arithmetic: 8.99 us -> 0 us
    all_gather x1 -> x0, waiting for transfers between devices: 149 us -> none  [local(): block_rows = lax.all_gather(normed, 'member', axis=1, tiled=True)]
    psum x1 -> x0, blocking collectives: 68.9 us -> none  [local(): summed, counted = lax.psum((summed, counted), ('group', 'member'))]
    pallas_call x0 -> x1, Pallas kernels: none -> 61.8 us  [local(): pl.pallas_call(functools.partial(kernel, groups), out_shape=jax.ShapeDtyp...]
    dot_general x1 -> x0, matrix products: 24.1 us -> none  [local(): jnp.einsum('csd,cpd->csp', normed, block_rows, preferred_element_type=jnp...]
    all_gather x1 -> x0, blocking collectives: 18.6 us -> none  [local(): all_ranks = lax.all_gather(order_rank, 'member', axis=1, tiled=True)]
    reduce_sum x3 -> x0, other arithmetic: 5.79 us -> none  [the longest x1 2.22 us: local(): jnp.sum(shifted * shifted, axis=-1, keepdims=True) + 1e-06]
  transfers between devices with their start and end apart: 1 -> 0, of which waited for: 1 -> 0; matrix products, arithmetic and copies ran while one was open for 0% -> 0% of each run, Pallas kernels for 0% -> 0%
where the time goes in v1:
time: 63.3 us; the launch traced here: 63.1 us
  Pallas kernels  61.8 us (98%)
  local copies, waits for them, and re-layouts  1.28 us (2%)
    pallas_call x1, Pallas kernels, local(): pl.pallas_call(functools.partial(kernel, groups), out_shape=jax.ShapeDtyp...  61.8 us
    unnamed x1, local copies, waits for them, and re-layouts  1.28 us

profile of v1, /device:TPU:1, one launch (start us, length us, event | category | flops | bytes accessed | tf_op | source)
XLA Modules:
  0.0 63.1 jit_solution(7507694338155271055)
XLA Ops:
  0.0 61.8 %shard_map.37 = f32[2,512]{1,0:T(2,128)} custom-call(s32[2]{0:T(128)} %lengths_hbm.1, bf16[2,4,128,1024]{3,2,1,0:T(8,128)(2,1)} %bitcast.1, s32[2,512]{1,0:T(2,128)} %order_hbm.1), custom_call_target="tpu_custom_call" | custom-call | flops 10000000000 | bytes 4000000 | tf_op jit(solution)/shard_map/pallas_call | solution.py:459
  61.8 1.3 %copy.5 = f32[2,512]{1,0:T(2,128)} copy(f32[2,512]{1,0:T(2,128)} %shard_map.37) | data formatting | bytes 8192

commit v2 on v1

--- a/solution.py
+++ b/solution.py
@@ -1,5 +1,3 @@
-import functools
-
 import jax
 import jax.numpy as jnp
 from jax import lax
@@ -14,7 +12,8 @@
 LP, LQ, LR = 4, 10, 16
 OTHER = 22
 NO_RANK = 1e9
-FILL, BULK = 8, 12
+AHEAD = 2
+LEAVE = 8
 WIDE = 4
 NONE = -1
 
@@ -47,18 +46,23 @@
     def there(unit):
         return 0 if unit < LP else (unit - LP) % STEPS + 1
 
-    todo = sorted(needed(role), key=lambda job: max(there(job[0] + 1), there(job[1])))
     ready = lambda job: max(there(job[0] + 1), there(job[1]))
+    todo = sorted(needed(role), key=ready)
     plan, at = [], 0
-    for stage in range(STEPS + 1):
-        for limit, cap in ((stage - 1, FILL), (stage, BULK)):
-            if stage == STEPS:
-                cap = len(todo)
-            take = []
-            while at < len(todo) and ready(todo[at]) <= limit and len(take) < cap:
-                take.append(todo[at])
-                at += 1
-            plan.append(take)
+
+    def take(limit, leave):
+        nonlocal at
+        able = sum(ready(job) <= limit for job in todo)
+        until = max(at, able - leave)
+        plan.append(todo[at:until])
+        at = until
+
+    take(0, 0)
+    for s in range(AHEAD):
+        take(s + 1, LEAVE if s == AHEAD - 1 else 0)
+    for s in range(AHEAD, STEPS):
+        take(s, 0)
+        take(s + 1, LEAVE if s < STEPS - 1 else 0)
     return plan
 
 
@@ -70,8 +74,8 @@
 
 
 def kernel(
-    groups, lengths_hbm, emb, order_hbm, out, lengths, order, raw, norm, cranks, rranks, rowacc, colacc, sums, totals, ret, back, center,
-    load_sem, raw_send, raw_recv, core_send, core_recv, sum_send, sum_recv, total_send, total_recv, ret_send, ret_recv,
+    lengths_hbm, emb, order_hbm, out, lengths, order, raw, norm, cranks, rranks, rowacc, colacc, sums, parts, tiles, ret, back, center,
+    load_sem, raw_send, raw_recv, core_send, core_recv, sum_send, sum_recv, part_send, part_recv, tile_send, tile_recv, ret_send, ret_recv,
 ):
     group, member = lax.axis_index("group"), lax.axis_index("member")
     core, x, y = member % 2, (member // 2) % 4, member // 8
@@ -98,6 +102,7 @@
         pick(role, (LR, LP, LR, LQ)),
     ]
     late_pair = role >= 2
+    is_c = role == 1
 
     small = [
         pltpu.make_async_copy(lengths_hbm, lengths, load_sem.at[2]),
@@ -110,13 +115,21 @@
         loads.append(pltpu.make_async_copy(emb.at[cluster], raw.at[pl.ds(first, PER)], load_sem.at[i]))
         loads[-1].start()
     barrier = pltpu.get_barrier_semaphore()
-    for i in range(1, 16):
-        pl.semaphore_signal(barrier, inc=1, device_id={"member": (member + i) % 16}, device_id_type=MESH)
-    for i in range(1, groups):
-        pl.semaphore_signal(barrier, inc=1, device_id={"group": (group + i) % groups}, device_id_type=MESH)
-
-    rowacc[...] = jnp.full(rowacc.shape, -1.0, jnp.float32)
-    colacc[...] = jnp.full(colacc.shape, -1.0, jnp.float32)
+    z, wide_y = group % 4, 2 * (group // 4) + y
+
+    def along(axis, i):
+        if axis == 0:
+            return {"group": 4 * (group // 4) + (z + i) % 4, "member": member}
+        if axis == 1:
+            to = (wide_y + i) % 4
+            return {"group": 4 * (to // 2) + z, "member": 8 * (to % 2) + 2 * x + core}
+        return {"group": group, "member": 8 * y + 2 * ((x + i) % 4) + core}
+
+    for axis in range(3):
+        for i in range(1, 4):
+            pl.semaphore_signal(barrier, inc=1, device_id=along(axis, i), device_id_type=MESH)
+    pl.semaphore_signal(barrier, inc=1, device_id=sibling, device_id_type=MESH)
+
     ret[...] = jnp.full(ret.shape, -1.0, jnp.float32)
     back[...] = jnp.full(back.shape, -1.0, jnp.float32)
 
@@ -131,7 +144,11 @@
             own_live.append(is_live)
             own = order[c : c + 1, i * UNIT : (i + 1) * UNIT].astype(jnp.float32)
             own_ranks.append(jnp.where(is_live, own, NO_RANK))
-    sums[member, 16:24, :] = jnp.concatenate(own_ranks, axis=0)
+    by_cluster = [jnp.concatenate(own_ranks[PER * c : PER * (c + 1)], axis=0) for c in range(2)]
+    first = mine == 0
+    sums[core, 16:24, :] = jnp.concatenate(
+        [jnp.where(first, by_cluster[0], by_cluster[1]), jnp.where(first, by_cluster[1], by_cluster[0])], axis=0
+    )
 
     for cp in loads:
         cp.wait()
@@ -152,25 +169,17 @@
     total = jnp.sum(total, axis=0, keepdims=True)
     rows_out = [total[:, 128 * i : 128 * (i + 1)] for i in range(8)]
     rows_out += [jnp.broadcast_to(count, (1, 128))] + [jnp.zeros((7, 128), jnp.float32)]
-    sums[member, 0:16, :] = jnp.concatenate(rows_out, axis=0)
-
-    pl.semaphore_wait(barrier, 15 + groups - 1)
-
-    def to_member(buffer, send, recv, i):
-        return pltpu.make_async_remote_copy(
-            src_ref=buffer.at[member], dst_ref=buffer.at[member], send_sem=send.at[i], recv_sem=recv.at[member],
-            device_id={"member": (member + i) % 16}, device_id_type=MESH,
-        )
-
-    def from_member(buffer, send, recv, i):
-        source = (member + 16 - i) % 16
-        return pltpu.make_async_remote_copy(
-            src_ref=buffer.at[source], dst_ref=buffer.at[source], send_sem=send.at[i], recv_sem=recv.at[source],
-            device_id={"member": (member + i) % 16}, device_id_type=MESH,
-        )
-
-    for i in range(1, 16):
-        to_member(sums, sum_send, sum_recv, i).start()
+    sums[core, 0:16, :] = jnp.concatenate(rows_out, axis=0)
+
+    pl.semaphore_wait(barrier, 10)
+
+    def with_sibling(slot):
+        return pltpu.make_async_remote_copy(
+            src_ref=sums.at[slot], dst_ref=sums.at[slot], send_sem=sum_send.at[0], recv_sem=sum_recv.at[0],
+            device_id=sibling, device_id_type=MESH,
+        )
+
+    with_sibling(core).start()
 
     def source_of(link, s):
         if link == 0:
@@ -210,7 +219,10 @@
         else:
             pl.when(condition)(do)
 
-    is_c = role == 1
+    def held(link, s):
+        if link == 0 and s < 2:
+            return jnp.logical_not(late_pair)
+        return comes(link, s)
 
     def send_step(s, everyone):
         for link in range(3):
@@ -218,10 +230,6 @@
             guarded(condition, lambda link=link: outgoing(link, s).start())
 
     def forward(s):
-        if s == 0:
-            send_step(1, True)
-        if s + 2 < 4:
-            send_step(s + 2, False)
         if s in (2, 3):
 
             @pl.when(late_pair)
@@ -242,57 +250,90 @@
         forward(s)
 
     send_step(0, True)
-
-    for i in range(1, 16):
-        from_member(sums, sum_send, sum_recv, i).wait_recv()
-    totals[group] = jnp.sum(sums[:, 0:16, :], axis=0)
-
-    def across(i, source):
-        at = (group + groups - i) % groups if source else group
-        return pltpu.make_async_remote_copy(
-            src_ref=totals.at[at], dst_ref=totals.at[at], send_sem=total_send.at[i], recv_sem=total_recv.at[at],
-            device_id={"group": (group + i) % groups}, device_id_type=MESH,
-        )
-
-    for i in range(1, groups):
-        across(i, False).start()
-
-    def owner_of(link, s):
+    rowacc[...] = jnp.full(rowacc.shape, -1.0, jnp.float32)
+    colacc[...] = jnp.full(colacc.shape, -1.0, jnp.float32)
+
+    with_sibling(1 - core).wait_recv()
+    place = (z, wide_y, x)
+
+    def part(axis, i, source):
+        at = (place[axis] + 4 - i) % 4 if source else place[axis]
+        return pltpu.make_async_remote_copy(
+            src_ref=parts.at[axis, at], dst_ref=parts.at[axis, at], send_sem=part_send.at[axis, i], recv_sem=part_recv.at[axis, at],
+            device_id=along(axis, i), device_id_type=MESH,
+        )
+
+    def spread(axis, value):
+        parts[axis, place[axis]] = value
+        for i in range(1, 4):
+            part(axis, i, False).start()
+
+    def gathered(axis):
+        for i in range(1, 4):
+            part(axis, i, True).wait_recv()
+        return (parts[axis, 0] + parts[axis, 1]) + (parts[axis, 2] + parts[axis, 3])
+
+    spread(0, sums[0, 0:16, :] + sums[1, 0:16, :])
+
+    for i in range(2):
+        lines = slice(16 + 4 * i, 20 + 4 * i)
+        tiles[i] = jnp.concatenate([sums[0, lines, :], sums[1, lines, :]], axis=0)
+    far_link = [pick(role, (0, 0, 1, 2)), pick(role, (2, 0, 1, 1)), pick(role, (2, 0, 2, 1))]
+
+    def give_tile(link, again):
+        if not again:
+            source = 0 if link == 0 else 1
+        elif link == 0:
+            source = 6
+        else:
+            source = jnp.where(is_c, 6 if link == 1 else 4, 2)
+        landed = 2 + 2 * far_link[link] + again
+        return pltpu.make_async_remote_copy(
+            src_ref=tiles.at[source], dst_ref=tiles.at[landed], send_sem=tile_send.at[link, again], recv_sem=tile_recv.at[landed],
+            device_id={"member": 2 * neighbour[link] + core}, device_id_type=MESH,
+        )
+
+    def take_tile(link, again):
+        at = 2 + 2 * link + again
+        return pltpu.make_async_remote_copy(
+            src_ref=tiles.at[at], dst_ref=tiles.at[at], send_sem=tile_send.at[link, again], recv_sem=tile_recv.at[at],
+            device_id={"member": 2 * neighbour[link] + core}, device_id_type=MESH,
+        )
+
+    for link in range(3):
+        give_tile(link, 0).start()
+
+    spread(1, gathered(0))
+    send_step(1, True)
+    for link in range(3):
+        take_tile(link, 0).wait_recv()
+    for link in range(3):
+        guarded(goes(link, 4), lambda link=link: give_tile(link, 1).start())
+    spread(2, gathered(1))
+    send_step(2, False)
+
+    def line_of(link, s):
         if link == 0:
-            return actual(pick(role, (1, 0, 5, 2))), (s - 2 * jnp.where(late_pair, 1, 0))
+            return 2 + jnp.where(late_pair, 1, 0), s - 2 * jnp.where(late_pair, 1, 0)
         if link == 1:
-            if s < 4:
-                return actual(pick(role, (3, 2, 3, 4))), s
-            return actual(pick(role, (7, 6, 7, 7))), s - 4 + 2 * is_m
-        if s < 4:
-            return actual(pick(role, (4, 5, 6, 6))), (s + 2 * is_m) % 4
-        return actual(pick(role, (7, 6, 7, 7))), s - 2
-
-    def set_ranks(unit, owner, at):
-        line = 4 * mine + at
-        both = [sums[2 * owner + j, pl.ds(16 + line, 1), :] for j in range(2)]
+            return (4, s) if s < 4 else (5, s - 4 + 2 * is_m)
+        return (6, (s + 2 * is_m) % 4) if s < 4 else (7, s - 2)
+
+    def set_ranks(unit, tile, at):
+        both = [tiles[tile, pl.ds(4 * j + at, 1), :] for j in range(2)]
         cranks[unit] = jnp.concatenate(both, axis=1)
-        own = sums[2 * owner + core, pl.ds(16 + line, 1), :]
+        own = tiles[tile, pl.ds(4 * core + at, 1), :]
         rranks[unit] = jnp.broadcast_to(own, (UNIT, UNIT)).T
 
-    arrive(0)
     for i in range(PER):
-        set_ranks(i, chip, i)
+        set_ranks(i, 0, i)
     for link in range(3):
+        guarded(comes(link, 4), lambda link=link: take_tile(link, 1).wait_recv())
         for s in range(STEPS):
-            unit = bases[link] + s
-
-            def one(link=link, s=s, unit=unit):
-                set_ranks(unit, *owner_of(link, s))
-
-            condition = comes(link, s)
-            if link == 0 and s < 2:
-                condition = jnp.logical_not(late_pair)
-            guarded(condition, one)
-
-    for i in range(1, groups):
-        across(i, True).wait_recv()
-    whole = jnp.sum(totals[...], axis=0)
+            guarded(held(link, s), lambda link=link, s=s: set_ranks(bases[link] + s, *line_of(link, s)))
+
+    whole = gathered(2)
+    send_step(3, False)
     mean = whole[0:8] / whole[8:9]
     center[...] = jnp.concatenate([mean[i : i + 1] for i in range(8)], axis=1)
 
@@ -350,29 +391,34 @@
 
         lax.fori_loop(0, pick(role, [len(jobs) // WIDE for jobs in lists]), body, 0)
 
-    def held(link, s):
-        if link == 0 and s < 2:
-            return jnp.logical_not(late_pair)
-        return comes(link, s)
-
     def own_unit(unit, _):
         prepare(unit)
         return 0
 
     lax.fori_loop(0, PER, own_unit, 0)
-    arrive(1)
+
+    def prepare_step(s):
+        arrive(s)
+        for link in range(3):
+            guarded(held(link, s), lambda link=link: prepare(bases[link] + s))
+
+    def exchanged(s):
+        for link in range(3):
+            guarded(held(link, s), lambda link=link: exchange(bases[link] + s, theirs).wait_recv())
+
+    for s in range(AHEAD):
+        prepare_step(s)
     for i in range(PER):
         exchange(i, theirs).wait_recv()
-    run_jobs(1)
-    for s in range(STEPS):
-        if s > 1:
-            arrive(s)
-        for link in range(3):
-            guarded(held(link, s), lambda link=link: prepare(bases[link] + s))
-        run_jobs(2 * s + 2)
-        for link in range(3):
-            guarded(held(link, s), lambda link=link: exchange(bases[link] + s, theirs).wait_recv())
-        run_jobs(2 * s + 3)
+    run_jobs(0)
+    for s in range(AHEAD):
+        exchanged(s)
+        run_jobs(1 + s)
+    for s in range(AHEAD, STEPS):
+        prepare_step(s)
+        run_jobs(1 + AHEAD + 2 * (s - AHEAD))
+        exchanged(s)
+        run_jobs(2 + AHEAD + 2 * (s - AHEAD))
 
     def finish(unit, slot, at):
         best = jnp.max(colacc[unit], axis=0, keepdims=True)
@@ -384,8 +430,13 @@
     for link in range(3):
         for s in range(STEPS):
             slot = 1 + link if s < 4 or link == 0 else 4
-            guarded(held(link, s), lambda link=link, s=s, slot=slot: finish(bases[link] + s, slot, owner_of(link, s)[1]))
-    owners = [owner_of(0, 2)[0], owner_of(1, 0)[0], owner_of(2, 0)[0], owner_of(1, 4)[0]]
+            guarded(held(link, s), lambda link=link, s=s, slot=slot: finish(bases[link] + s, slot, line_of(link, s)[1]))
+    owners = [
+        actual(pick(role, (1, 0, 5, 2))),
+        actual(pick(role, (3, 2, 3, 4))),
+        actual(pick(role, (4, 5, 6, 6))),
+        actual(pick(role, (7, 6, 7, 7))),
+    ]
 
     def give(slot, j):
         return pltpu.make_async_remote_copy(
@@ -431,10 +482,14 @@
         for i in range(PER):
             out[c : c + 1, i * UNIT : (i + 1) * UNIT] = jnp.where(own_live[c * PER + i], best[i : i + 1], -1.0)
 
-    for i in range(1, 16):
-        to_member(sums, sum_send, sum_recv, i).wait_send()
-    for i in range(1, groups):
-        across(i, False).wait_send()
+    with_sibling(core).wait_send()
+    for link in range(3):
+        give_tile(link, 0).wait_send()
+        guarded(goes(link, 4), lambda link=link: give_tile(link, 1).wait_send())
+
+    for axis in range(3):
+        for i in range(1, 4):
+            part(axis, i, False).wait_send()
     for s in range(STEPS):
         for link in range(3):
             guarded(goes(link, s), lambda link=link: outgoing(link, s).wait_send())
@@ -450,14 +505,13 @@
 
 
 def solution(mesh):
-    groups = mesh.shape["group"]
     units = LR + STEPS
 
     def local(embeddings, order_rank, lengths):
         d = embeddings.shape[-1]
         f32, dma = jnp.float32, pltpu.SemaphoreType.DMA
         return pl.pallas_call(
-            functools.partial(kernel, groups),
+            kernel,
             out_shape=jax.ShapeDtypeStruct(order_rank.shape, f32),
             in_specs=[
                 pl.BlockSpec(memory_space=pl.ANY),
@@ -474,8 +528,9 @@
                 pltpu.VMEM((units, UNIT, UNIT), f32),
                 pltpu.VMEM((units, UNIT, UNIT), f32),
                 pltpu.VMEM((units, 8, 2 * UNIT), f32),
-                pltpu.VMEM((16, 24, UNIT), f32),
-                pltpu.VMEM((groups, 16, UNIT), f32),
+                pltpu.VMEM((2, 24, UNIT), f32),
+                pltpu.VMEM((3, 4, 16, UNIT), f32),
+                pltpu.VMEM((8, 8, UNIT), f32),
                 pltpu.VMEM((5, 2, 8, UNIT), f32),
                 pltpu.VMEM((16, 8, UNIT), f32),
                 pltpu.VMEM((1, d), f32),
@@ -484,10 +539,12 @@
                 dma((3 * STEPS,)),
                 dma((units,)),
                 dma((units,)),
-                dma((16,)),
-                dma((16,)),
-                dma((groups,)),
-                dma((groups,)),
+                dma((1,)),
+                dma((1,)),
+                dma((3, 4)),
+                dma((3, 4)),
+                dma((3, 2)),
+                dma((8,)),
                 dma((5, 2)),
                 dma((16,)),
             ],

time: 63.3 us -> 57.5 us (0.908)
  Pallas kernels: 61.8 us -> 56.1 us
    pallas_call x1, Pallas kernels: 61.8 us -> 56.1 us  [local(): pl.pallas_call(kernel, out_shape=jax.ShapeDtypeStruct(order_rank.shape, f...]
where the time goes in v2:
time: 57.5 us; the launch traced here: 57.4 us
  Pallas kernels  56.1 us (98%)
  local copies, waits for them, and re-layouts  1.28 us (2%)
    pallas_call x1, Pallas kernels, local(): pl.pallas_call(kernel, out_shape=jax.ShapeDtypeStruct(order_rank.shape, f...  56.1 us
    unnamed x1, local copies, waits for them, and re-layouts  1.28 us

profile of v2, /device:TPU:1, one launch (start us, length us, event | category | flops | bytes accessed | tf_op | source)
XLA Modules:
  0.0 57.4 jit_solution(18055993988223496898)
XLA Ops:
  0.0 56.1 %shard_map.37 = f32[2,512]{1,0:T(2,128)} custom-call(s32[2]{0:T(128)} %lengths_hbm.1, bf16[2,4,128,1024]{3,2,1,0:T(8,128)(2,1)} %bitcast.1, s32[2,512]{1,0:T(2,128)} %order_hbm.1), custom_call_target="tpu_custom_call" | custom-call | flops 10000000000 | bytes 4000000 | tf_op jit(solution)/shard_map/pallas_call | solution.py:513
  56.1 1.3 %copy.5 = f32[2,512]{1,0:T(2,128)} copy(f32[2,512]{1,0:T(2,128)} %shard_map.37) | data formatting | bytes 8192

commit v3 on v2

--- a/solution.py
+++ b/solution.py
@@ -13,8 +13,8 @@
 OTHER = 22
 NO_RANK = 1e9
 AHEAD = 2
-LEAVE = 8
-WIDE = 4
+LEAVE, LAST_LEAVE = 4, 4
+WIDE, LAST_WIDE = 4, 7
 NONE = -1
 
 
@@ -62,7 +62,7 @@
         take(s + 1, LEAVE if s == AHEAD - 1 else 0)
     for s in range(AHEAD, STEPS):
         take(s, 0)
-        take(s + 1, LEAVE if s < STEPS - 1 else 0)
+        take(s + 1, 0 if s == STEPS - 1 else LAST_LEAVE if s == STEPS - 2 else LEAVE)
     return plan
 
 
@@ -224,8 +224,8 @@
             return jnp.logical_not(late_pair)
         return comes(link, s)
 
-    def send_step(s, everyone):
-        for link in range(3):
+    def send_step(s, everyone, links=(0, 1, 2)):
+        for link in links:
             condition = None if everyone or link == 0 else jnp.logical_not(is_c)
             guarded(condition, lambda link=link: outgoing(link, s).start())
 
@@ -237,16 +237,15 @@
                 for link in range(3):
                     outgoing(link, s + 2).start()
 
-        if s < 4:
-
-            @pl.when(is_c)
-            def _():
-                for link in (1, 2):
-                    outgoing(link, s + 2).start()
-
     def arrive(s):
-        for link in range(3):
+        for link in (2, 1, 0):
             guarded(comes(link, s), lambda link=link: arriving(link, s).wait_recv())
+            if s < 4 and link:
+
+                @pl.when(is_c)
+                def _():
+                    outgoing(3 - link, s + 2).start()
+
         forward(s)
 
     send_step(0, True)
@@ -332,8 +331,10 @@
         for s in range(STEPS):
             guarded(held(link, s), lambda link=link, s=s: set_ranks(bases[link] + s, *line_of(link, s)))
 
+    send_step(3, False, (1, 2))
+    arrive(0)
     whole = gathered(2)
-    send_step(3, False)
+    send_step(3, False, (0,))
     mean = whole[0:8] / whole[8:9]
     center[...] = jnp.concatenate([mean[i : i + 1] for i in range(8)], axis=1)
 
@@ -370,8 +371,8 @@
 
     plans = [jobs_of(r) for r in range(3)]
 
-    def run_jobs(part):
-        lists = [plan[part] + plan[part][-1:] * (-len(plan[part]) % WIDE) for plan in plans]
+    def run_jobs(part, wide=WIDE):
+        lists = [plan[part] + plan[part][-1:] * (-len(plan[part]) % wide) for plan in plans]
         lists.append(lists[2])
         longest = max(len(jobs) for jobs in lists)
         if not longest:
@@ -382,23 +383,25 @@
             codes.append(pick(role, at))
 
         def body(j, _):
-            for k in range(WIDE):
+            for k in range(wide):
                 code = codes[k]
-                for i in range(1, longest // WIDE):
-                    code = jnp.where(j == i, codes[WIDE * i + k], code)
+                for i in range(1, longest // wide):
+                    code = jnp.where(j == i, codes[wide * i + k], code)
                 pair(code // 32, code % 32)
             return 0
 
-        lax.fori_loop(0, pick(role, [len(jobs) // WIDE for jobs in lists]), body, 0)
+        lax.fori_loop(0, pick(role, [len(jobs) // wide for jobs in lists]), body, 0)
 
     def own_unit(unit, _):
         prepare(unit)
         return 0
 
+    arrive(1)
     lax.fori_loop(0, PER, own_unit, 0)
 
     def prepare_step(s):
-        arrive(s)
+        if s > 1:
+            arrive(s)
         for link in range(3):
             guarded(held(link, s), lambda link=link: prepare(bases[link] + s))
 
@@ -418,7 +421,7 @@
         prepare_step(s)
         run_jobs(1 + AHEAD + 2 * (s - AHEAD))
         exchanged(s)
-        run_jobs(2 + AHEAD + 2 * (s - AHEAD))
+        run_jobs(2 + AHEAD + 2 * (s - AHEAD), LAST_WIDE if s == STEPS - 1 else WIDE)
 
     def finish(unit, slot, at):
         best = jnp.max(colacc[unit], axis=0, keepdims=True)
@@ -427,10 +430,6 @@
             part = best[:, UNIT * j : UNIT * (j + 1)]
             ret[slot, j, pl.ds(at, 1), :] = jnp.where(core == j, jnp.maximum(part, across_lanes), part)
 
-    for link in range(3):
-        for s in range(STEPS):
-            slot = 1 + link if s < 4 or link == 0 else 4
-            guarded(held(link, s), lambda link=link, s=s, slot=slot: finish(bases[link] + s, slot, line_of(link, s)[1]))
     owners = [
         actual(pick(role, (1, 0, 5, 2))),
         actual(pick(role, (3, 2, 3, 4))),
@@ -444,7 +443,11 @@
             device_id={"member": 2 * owners[slot - 1] + j}, device_id_type=MESH,
         )
 
-    for slot in range(1, 5):
+    slots = [[(link, s) for s in range(STEPS) if s < 4 or link == 0] for link in range(3)]
+    slots.append([(link, s) for link in (1, 2) for s in (4, 5)])
+    for slot in (4, 1, 2, 3):
+        for link, s in slots[slot - 1]:
+            guarded(held(link, s), lambda link=link, s=s, slot=slot: finish(bases[link] + s, slot, line_of(link, s)[1]))
         for j in range(2):
             give(slot, j).start()
     for i in range(PER):

time: 57.5 us -> 55.5 us (0.965)
  Pallas kernels: 56.1 us -> 54 us
    pallas_call x1, Pallas kernels: 56.1 us -> 54 us  [local(): pl.pallas_call(kernel, out_shape=jax.ShapeDtypeStruct(order_rank.shape, f...]
where the time goes in v3:
time: 55.5 us; the launch traced here: 55.3 us
  Pallas kernels  54 us (97%)
  local copies, waits for them, and re-layouts  1.28 us (2%)
    pallas_call x1, Pallas kernels, local(): pl.pallas_call(kernel, out_shape=jax.ShapeDtypeStruct(order_rank.shape, f...  54 us
    unnamed x1, local copies, waits for them, and re-layouts  1.28 us

profile of v3, /device:TPU:1, one launch (start us, length us, event | category | flops | bytes accessed | tf_op | source)
XLA Modules:
  0.0 55.3 jit_solution(2696620449703294380)
XLA Ops:
  0.0 54.0 %shard_map.37 = f32[2,512]{1,0:T(2,128)} custom-call(s32[2]{0:T(128)} %lengths_hbm.1, bf16[2,4,128,1024]{3,2,1,0:T(8,128)(2,1)} %bitcast.1, s32[2,512]{1,0:T(2,128)} %order_hbm.1), custom_call_target="tpu_custom_call" | custom-call | flops 10000000000 | bytes 4000000 | tf_op jit(solution)/shard_map/pallas_call | solution.py:516
  54.0 1.3 %copy.5 = f32[2,512]{1,0:T(2,128)} copy(f32[2,512]{1,0:T(2,128)} %shard_map.37) | data formatting | bytes 8192

commit v4 on v3

--- a/solution.py
+++ b/solution.py
@@ -14,7 +14,7 @@
 NO_RANK = 1e9
 AHEAD = 2
 LEAVE, LAST_LEAVE = 4, 4
-WIDE, LAST_WIDE = 4, 7
+WIDE, LAST_WIDE = 4, 14
 NONE = -1
 
 

time: 55.5 us -> 55.4 us (level)
  no operation moved by 1% of the time
where the time goes in v4:
time: 55.4 us; the launch traced here: 55.2 us
  Pallas kernels  53.9 us (97%)
  local copies, waits for them, and re-layouts  1.28 us (2%)
    pallas_call x1, Pallas kernels, local(): pl.pallas_call(kernel, out_shape=jax.ShapeDtypeStruct(order_rank.shape, f...  53.9 us
    unnamed x1, local copies, waits for them, and re-layouts  1.28 us

profile of v4, /device:TPU:1, one launch (start us, length us, event | category | flops | bytes accessed | tf_op | source)
XLA Modules:
  0.0 55.2 jit_solution(7813946371498821343)
XLA Ops:
  0.0 53.9 %shard_map.37 = f32[2,512]{1,0:T(2,128)} custom-call(s32[2]{0:T(128)} %lengths_hbm.1, bf16[2,4,128,1024]{3,2,1,0:T(8,128)(2,1)} %bitcast.1, s32[2,512]{1,0:T(2,128)} %order_hbm.1), custom_call_target="tpu_custom_call" | custom-call | flops 10000000000 | bytes 4000000 | tf_op jit(solution)/shard_map/pallas_call | solution.py:516
  53.9 1.3 %copy.5 = f32[2,512]{1,0:T(2,128)} copy(f32[2,512]{1,0:T(2,128)} %shard_map.37) | data formatting | bytes 8192
